TPU v7x, 32 devices: a whole 2x2x4 slice. The times are simulated.
32 devices in a mesh: grp: 4 (over x, core), blk: 8 (over z, y).
Axes of the slice: x: 2, y: 2, z: 4, core: 2. Of those that a mesh axis runs over, the one named last changes fastest.
Arguments:
- image_embeds: bfloat16 [8192, 1152], P(('grp', 'blk')), may hold values from -6 to 6
- text_embeds: bfloat16 [8192, 1152], P(('grp', 'blk')), may hold values from -6 to 6
- positives: int32 [32, 256], P(('grp', 'blk')), may hold values from 0 to 255, each once within a row
- logit_scale: float32 [1], replicated, may hold values from 60 to 150
- logit_bias: float32 [1], replicated, may hold values from -4 to -1
Outputs:
- image_grad: float32 [8192, 1152], P(('grp', 'blk'))
- text_grad: float32 [8192, 1152], P(('grp', 'blk'))
Inputs may be any that keep to these rules, and one draw needn't show every extreme that they name: Each row of positives names every position of its block once, so each image of a block has its own matching text.
All inputs are finite; a program needn't handle non-finite values.
Results may differ from a plain program's by a relative error of at most 0.0055.
Values may be sent and summed in bfloat16 or wider, within the bound.
A program may use at most 64 MiB of HBM per device.

v0:
```python
import jax
import jax.numpy as jnp
from jax import lax
from jax.sharding import PartitionSpec as P

STEPS = 4


def partner(value, axis, distance):
    mask = 2**distance
    pairs = [(source, source ^ mask) for source in range(lax.axis_size(axis))]
    return lax.ppermute(value, axis, pairs)


def shifted(value, axis, steps):
    count = lax.axis_size(axis)
    pairs = [(source, (source + steps) % count) for source in range(count)]
    return lax.ppermute(value, axis, pairs)


def unit_rows(embeds):
    values = embeds.astype(jnp.float32)
    inverse = lax.rsqrt(jnp.sum(values * values, axis=-1, keepdims=True) + 1e-06)
    return (values, inverse, (values * inverse).astype(jnp.bfloat16))


def unit_back(values, inverse, grad_unit):
    projection = jnp.sum(values * grad_unit, axis=-1, keepdims=True)
    return inverse * grad_unit - inverse * inverse * inverse * values * projection


def pair_coef(image_rows, text_rows, label_cols, scale_value, bias_value, holds_positive):
    products = lax.dot_general(
        image_rows, text_rows, (((1,), (1,)), ((), ())), preferred_element_type=jnp.float32
    )
    logits = scale_value * products + bias_value
    if holds_positive:
        columns = lax.broadcasted_iota(jnp.int32, logits.shape, 1)
        label_sign = jnp.where(columns == label_cols[:, None], 1.0, -1.0).astype(jnp.float32)
    else:
        label_sign = -1.0
    return (-label_sign * scale_value * jax.nn.sigmoid(-label_sign * logits)).astype(jnp.bfloat16)


def column_product(coefficient, rows):
    return lax.dot_general(
        coefficient, rows, (((0,), (0,)), ((), ())), preferred_element_type=jnp.float32
    )


def on_device(image_embeds, text_embeds, positives, logit_scale, logit_bias):
    image_values, image_inverse, image_unit = unit_rows(image_embeds)
    text_values, text_inverse, text_unit = unit_rows(text_embeds)
    scale_value = logit_scale[0]
    bias_value = logit_bias[0]
    labels = positives[0]
    cycle_length = STEPS
    image_total = jnp.zeros(image_values.shape, jnp.float32)
    partner_text = partner(text_unit, "grp", 1)
    carried = jnp.stack([text_unit, partner_text])
    carried_grads = jnp.zeros(carried.shape, jnp.float32)
    for offset in range(cycle_length):
        new_grads = []
        for side_index in range(2):
            coefficient = pair_coef(
                image_unit,
                carried[side_index],
                labels,
                scale_value,
                bias_value,
                side_index == 0 and offset == 0,
            )
            image_total = image_total + jnp.dot(
                coefficient, carried[side_index], preferred_element_type=jnp.float32
            )
            new_grads.append(carried_grads[side_index] + column_product(coefficient, image_unit))
        carried_grads = jnp.stack(new_grads)
        if offset + 1 < cycle_length:
            carried = shifted(carried, "blk", 2)
            carried_grads = shifted(carried_grads, "blk", 2)
    returned = shifted(carried_grads, "blk", -2 * (cycle_length - 1))
    partner_grad = partner(returned[1], "grp", 1)
    text_total = returned[0] + partner_grad
    image_grad = unit_back(image_values, image_inverse, image_total)
    text_grad = unit_back(text_values, text_inverse, text_total)
    return (image_grad, text_grad)


def solution(mesh):
    return jax.shard_map(
        on_device,
        mesh=mesh,
        in_specs=(
            P(("grp", "blk"), None),
            P(("grp", "blk"), None),
            P(("grp", "blk"), None),
            P(),
            P(),
        ),
        out_specs=(P(("grp", "blk"), None), P(("grp", "blk"), None)),
        check_vma=False,
    )
```

profile of v0, /device:TPU:0, one launch (start us, length us, event | category | flops | bytes accessed | tf_op | source)
XLA Modules:
  0.0 338.6 jit_solution(6586633964053077861)
XLA Ops:
  0.6 1.3 fusion.8
  2.0 1.2 fusion.9
  3.2 3.0 collective-permute-start
  7.5 0.2 fusion.3
  7.7 0.4 fusion.75
  8.2 0.4 convolution_bitcast_fusion.1
  8.6 10.9 %collective-permute-done = bf16[256,1152]{1,0:T(8,128)(2,1)S(1)} collective-permute-done((bf16[256,1152]{1,0:T(8,128)(2,1)S(1)}, bf16[256,1152]{1,0:T(8,128)(2,1)S(1)}, u32[]{:S(2)}, u32[]{:S(2)}) %collective-permute-start) | collective-permute-done | bytes 589856 | tf_op jit(solution)/shard_map/ppermute | solution.py:12
  19.6 0.4 fusion.76
  20.0 0.4 convolution_bitcast_fusion
  20.4 0.2 pad_maximum_fusion
  20.6 1.9 collective-permute-start.4
  22.4 0.2 fusion.141
  22.6 0.1 pad_maximum_fusion.4
  22.7 1.6 collective-permute-start.1
  24.4 75.8 %collective-permute-done.1 = bf16[2,256,1152]{2,1,0:T(8,128)(2,1)S(1)} collective-permute-done((bf16[2,256,1152]{2,1,0:T(8,128)(2,1)S(1)}, bf16[2,256,1152]{2,1,0:T(8,128)(2,1)S(1)}, u32[]{:S(2)}, u32[]{:S(2)}) %collective-permute-start.1) | collective-permute-done | bytes 1179680 | tf_op jit(solution)/shard_map/ppermute | solution.py:18
  100.1 0.4 fusion.78
  100.6 0.4 fusion.77
  101.0 0.4 fusion.23
  101.4 0.4 fusion.25
  101.8 0.2 pad_maximum_fusion.1
  102.1 1.3 collective-permute-start.2
  103.3 77.3 %collective-permute-done.2 = bf16[2,256,1152]{2,1,0:T(8,128)(2,1)S(1)} collective-permute-done((bf16[2,256,1152]{2,1,0:T(8,128)(2,1)S(1)}, bf16[2,256,1152]{2,1,0:T(8,128)(2,1)S(1)}, u32[]{:S(2)}, u32[]{:S(2)}) %collective-permute-start.2) | collective-permute-done | bytes 1179680 | tf_op jit(solution)/shard_map/ppermute | solution.py:18
  180.6 0.4 fusion.80
  181.0 0.4 fusion.79
  181.4 0.4 fusion.19
  181.9 0.4 fusion.21
  182.3 0.2 pad_maximum_fusion.2
  182.6 77.5 %collective-permute-done.3 = bf16[2,256,1152]{2,1,0:T(8,128)(2,1)S(1)} collective-permute-done((bf16[2,256,1152]{2,1,0:T(8,128)(2,1)S(1)}, bf16[2,256,1152]{2,1,0:T(8,128)(2,1)S(1)}, u32[]{:S(2)}, u32[]{:S(2)}) %collective-permute-start.3) | collective-permute-done | bytes 1179680 | tf_op jit(solution)/shard_map/ppermute | solution.py:18
  260.1 0.4 fusion.82
  260.6 0.4 fusion.81
  261.0 0.4 fusion.15
  261.4 0.4 fusion.17
  261.8 0.2 pad_maximum_fusion.3
  262.1 0.3 fusion.120
  262.4 0.3 convolution_add_fusion.3
  262.8 0.3 fusion.83
  263.1 0.3 fusion
  263.5 0.3 fusion.84
  263.8 0.4 fusion.1
  264.2 49.3 %collective-permute-done.7 = f32[2,256,1152]{2,1,0:T(8,128)S(1)} collective-permute-done((f32[2,256,1152]{2,1,0:T(8,128)S(1)}, f32[2,256,1152]{2,1,0:T(8,128)S(1)}, u32[]{:S(2)}, u32[]{:S(2)}) %collective-permute-start.7) | collective-permute-done | bytes 2359328 | tf_op jit(solution)/shard_map/ppermute | solution.py:18
  313.5 0.1 slice_bitcast_fusion
  313.6 0.9 collective-permute-start.8
  314.5 0.3 fusion.85
  314.8 0.5 fusion.7
  315.3 1.3 fusion.6
  316.6 20.4 %collective-permute-done.8 = f32[256,1152]{1,0:T(8,128)S(1)} collective-permute-done((f32[256,1152]{1,0:T(8,128)S(1)}, f32[256,1152]{1,0:T(8,128)S(1)}, u32[]{:S(2)}, u32[]{:S(2)}) %collective-permute-start.8) | collective-permute-done | bytes 1179680 | tf_op jit(solution)/shard_map/ppermute | solution.py:12
  337.1 0.2 fusion.12
  337.3 1.3 fusion.11
  (15 shorter events, 0.3 us)
Async XLA Ops:
  0.6 6.9 %copy-start = (bf16[256,1152]{1,0:T(8,128)(2,1)S(1)}, bf16[256,1152]{1,0:T(8,128)(2,1)}, u32[]{:S(2)}) copy-start(bf16[256,1152]{1,0:T(8,128)(2,1)} %param.5) | copy-start | bytes 1769476
  0.6 7.1 %copy-start.2 = (s32[1,256]{1,0:T(1,128)S(1)}, s32[1,256]{1,0:T(1,128)}, u32[]{:S(2)}) copy-start(s32[1,256]{1,0:T(1,128)} %param.7) | copy-start | bytes 3076
  3.2 16.3 %collective-permute-start = (bf16[256,1152]{1,0:T(8,128)(2,1)S(1)}, bf16[256,1152]{1,0:T(8,128)(2,1)S(1)}, u32[]{:S(2)}, u32[]{:S(2)}) collective-permute-start(bf16[256,1152]{1,0:T(8,128)(2,1)S(1)} %fusion.9), channel_id=1, source_target_pairs={{0,16},{8,24},{16,0},{24,8},{1,17},{9,25},{17,1},{25,9},{2,18},{10... | collective-permute-start | bytes 1769480 | tf_op jit(solution)/shard_map/ppermute | solution.py:12
  20.4 2.1 copy-start.1
  20.6 80.4 %collective-permute-start.4 = (f32[2,256,1152]{2,1,0:T(8,128)S(1)}, f32[2,256,1152]{2,1,0:T(8,128)S(1)}, u32[]{:S(2)}, u32[]{:S(2)}) collective-permute-start(f32[2,256,1152]{2,1,0:T(8,128)S(1)} %pad_maximum_fusion), channel_id=1, source_target_pairs={{0,2},{1,3},{2,4},{3,5},{4,6},{5,7},{6,0},{7,1},{8,10},{9,11},{10,... | collective-permute-start | bytes 7077896 | tf_op jit(solution)/shard_map/ppermute | solution.py:18
  22.7 77.4 %collective-permute-start.1 = (bf16[2,256,1152]{2,1,0:T(8,128)(2,1)S(1)}, bf16[2,256,1152]{2,1,0:T(8,128)(2,1)S(1)}, u32[]{:S(2)}, u32[]{:S(2)}) collective-permute-start(bf16[2,256,1152]{2,1,0:T(8,128)(2,1)S(1)} %pad_maximum_fusion.4), channel_id=1, source_target_pairs={{0,2},{1,3},{2,4},{3,5},{4,6},{5,7},{6,0},{7,1},{8,10},{9,11},{10,... | collective-permute-start | bytes 3538952 | tf_op jit(solution)/shard_map/ppermute | solution.py:18
  102.0 79.4 %collective-permute-start.5 = (f32[2,256,1152]{2,1,0:T(8,128)S(1)}, f32[2,256,1152]{2,1,0:T(8,128)S(1)}, u32[]{:S(2)}, u32[]{:S(2)}) collective-permute-start(f32[2,256,1152]{2,1,0:T(8,128)S(1)} %pad_maximum_fusion.1), channel_id=1, source_target_pairs={{0,2},{1,3},{2,4},{3,5},{4,6},{5,7},{6,0},{7,1},{8,10},{9,11},{10,... | collective-permute-start | bytes 7077896 | tf_op jit(solution)/shard_map/ppermute | solution.py:18
  102.1 78.5 %collective-permute-start.2 = (bf16[2,256,1152]{2,1,0:T(8,128)(2,1)S(1)}, bf16[2,256,1152]{2,1,0:T(8,128)(2,1)S(1)}, u32[]{:S(2)}, u32[]{:S(2)}) collective-permute-start(bf16[2,256,1152]{2,1,0:T(8,128)(2,1)S(1)} %collective-permute-done.1), channel_id=1, source_target_pairs={{0,2},{1,3},{2,4},{3,5},{4,6},{5,7},{6,0},{7,1},{8,10},{9,11},{10,... | collective-permute-start | bytes 3538952 | tf_op jit(solution)/shard_map/ppermute | solution.py:18
  182.5 78.5 %collective-permute-start.6 = (f32[2,256,1152]{2,1,0:T(8,128)S(1)}, f32[2,256,1152]{2,1,0:T(8,128)S(1)}, u32[]{:S(2)}, u32[]{:S(2)}) collective-permute-start(f32[2,256,1152]{2,1,0:T(8,128)S(1)} %pad_maximum_fusion.2), channel_id=1, source_target_pairs={{0,2},{1,3},{2,4},{3,5},{4,6},{5,7},{6,0},{7,1},{8,10},{9,11},{10,... | collective-permute-start | bytes 7077896 | tf_op jit(solution)/shard_map/ppermute | solution.py:18
  182.5 77.6 %collective-permute-start.3 = (bf16[2,256,1152]{2,1,0:T(8,128)(2,1)S(1)}, bf16[2,256,1152]{2,1,0:T(8,128)(2,1)S(1)}, u32[]{:S(2)}, u32[]{:S(2)}) collective-permute-start(bf16[2,256,1152]{2,1,0:T(8,128)(2,1)S(1)} %collective-permute-done.2), channel_id=1, source_target_pairs={{0,2},{1,3},{2,4},{3,5},{4,6},{5,7},{6,0},{7,1},{8,10},{9,11},{10,... | collective-permute-start | bytes 3538952 | tf_op jit(solution)/shard_map/ppermute | solution.py:18
  262.0 51.5 %collective-permute-start.7 = (f32[2,256,1152]{2,1,0:T(8,128)S(1)}, f32[2,256,1152]{2,1,0:T(8,128)S(1)}, u32[]{:S(2)}, u32[]{:S(2)}) collective-permute-start(f32[2,256,1152]{2,1,0:T(8,128)S(1)} %pad_maximum_fusion.3), channel_id=1, source_target_pairs={{0,2},{1,3},{2,4},{3,5},{4,6},{5,7},{6,0},{7,1},{8,10},{9,11},{10,... | collective-permute-start | bytes 7077896 | tf_op jit(solution)/shard_map/ppermute | solution.py:18
  313.6 23.5 %collective-permute-start.8 = (f32[256,1152]{1,0:T(8,128)S(1)}, f32[256,1152]{1,0:T(8,128)S(1)}, u32[]{:S(2)}, u32[]{:S(2)}) collective-permute-start(f32[256,1152]{1,0:T(8,128)S(1)} %slice_bitcast_fusion), channel_id=1, source_target_pairs={{0,16},{8,24},{16,0},{24,8},{1,17},{9,25},{17,1},{25,9},{2,18},{10... | collective-permute-start | bytes 3538952 | tf_op jit(solution)/shard_map/ppermute | solution.py:12
where the time goes:
time: 339 us
  waiting for transfers between devices  311 us (92%)
  matrix products  9.65 us (3%)
  starting transfers between devices  8.92 us (3%)
  other arithmetic  6.55 us (2%)
    ppermute x7, waiting for transfers between devices, shifted(): return lax.ppermute(value, axis, pairs)  280 us
    ppermute x2, waiting for transfers between devices, partner(): return lax.ppermute(value, axis, pairs)  31.4 us
  transfers between devices with their start and end apart: 9, of which 6 were waited for; matrix products, arithmetic and copies ran while one was open for 2% of the time, Pallas kernels for 0%

commit v1 on v0

v1 whole, which is shorter than its diff:
```python
import functools

import jax
import jax.numpy as jnp
from jax import lax
from jax.experimental import pallas as pl
from jax.experimental.pallas import tpu as pltpu
from jax.sharding import PartitionSpec as P

STEPS = 4
CHUNKS = 4
MESH = pl.DeviceIdType.MESH


def partner(value, axis, distance):
    mask = 2**distance
    pairs = [(source, source ^ mask) for source in range(lax.axis_size(axis))]
    return lax.ppermute(value, axis, pairs)


def shifted(value, axis, steps):
    count = lax.axis_size(axis)
    pairs = [(source, (source + steps) % count) for source in range(count)]
    return lax.ppermute(value, axis, pairs)


def unit_rows(embeds):
    values = embeds.astype(jnp.float32)
    inverse = lax.rsqrt(jnp.sum(values * values, axis=-1, keepdims=True) + 1e-06)
    return (values, inverse, (values * inverse).astype(jnp.bfloat16))


def unit_back(values, inverse, grad_unit):
    projection = jnp.sum(values * grad_unit, axis=-1, keepdims=True)
    return inverse * grad_unit - inverse * inverse * inverse * values * projection


def dot_last(a, b):
    return lax.dot_general(a, b, (((1,), (1,)), ((), ())), preferred_element_type=jnp.float32)


def dot_first(a, b):
    return lax.dot_general(a, b, (((0,), (0,)), ((), ())), preferred_element_type=jnp.float32)


def window_plan(image_embeds, text_embeds, positives, logit_scale, logit_bias):
    image_values, image_inverse, image_unit = unit_rows(image_embeds)
    text_values, text_inverse, text_unit = unit_rows(text_embeds)
    scale, bias = logit_scale[0], logit_bias[0]
    rows = image_unit.shape[0]
    images = jnp.concatenate([image_unit, partner(image_unit, "grp", 1)])
    texts = [text_unit]
    for _ in range(STEPS - 1):
        texts.append(shifted(texts[-1], "blk", 2))
    image_total = jnp.zeros((2 * rows, image_unit.shape[1]), jnp.float32)
    text_parts = []
    for step in range(STEPS):
        logits = scale * dot_last(texts[step], images) + bias
        sign = jnp.full(logits.shape, -1.0, jnp.float32)
        if step == 0:
            places = lax.broadcasted_iota(jnp.int32, (rows, rows), 0)
            own = jnp.where(places == positives[0][None, :], 1.0, -1.0)
            sign = jnp.concatenate([own, sign[:, rows:]], axis=1)
        coefficient = (-sign * scale * jax.nn.sigmoid(-sign * logits)).astype(jnp.bfloat16)
        text_parts.append(
            jnp.dot(coefficient, images, preferred_element_type=jnp.float32)
        )
        image_total = image_total + dot_first(coefficient, texts[step])
    image_grad = image_total[:rows] + partner(image_total[rows:].astype(jnp.bfloat16), "grp", 1)
    text_total = text_parts[-1]
    for step in range(STEPS - 2, -1, -1):
        text_total = text_parts[step] + shifted(text_total.astype(jnp.bfloat16), "blk", -2)
    return (
        unit_back(image_values, image_inverse, image_grad),
        unit_back(text_values, text_inverse, text_total),
    )


def line_kernel(
    img_ref, txt_ref, pos_ref, scale_ref, bias_ref, img_out, txt_out,
    images, texts, coefs, parts, img_total, back, back_send, img_send, img_recv,
    i_sems, g_send, g_recv, r_send, r_recv, x_send, x_recv,
):
    rows, width = img_ref.shape
    piece = rows // CHUNKS
    last = STEPS - 1
    g = lax.axis_index("grp")
    b = lax.axis_index("blk")
    z = b // 2
    across = {"grp": g + 2 - 4 * ((g // 2) % 2)}
    scale = scale_ref[0]
    bias = bias_ref[0]

    def at(c):
        return pl.ds(pl.multiple_of(c * piece, piece), piece)

    def device(d):
        return {"blk": b + 2 * d}

    def has(d):
        return (z + d >= 0) & (z + d <= last)

    def side(d):
        return (d + 1) // 2

    def gather_copy(d, j, c):
        part = texts.at[j, at(c)]
        return pltpu.make_async_remote_copy(
            part, part, g_send.at[side(d), j, c], g_recv.at[j, c],
            device_id=device(d), device_id_type=MESH)

    def return_copy(d, j, c):
        return pltpu.make_async_remote_copy(
            back_send.at[j, at(c)], back.at[side(d), j, at(c)],
            r_send.at[side(d), j, c], r_recv.at[side(d), j, c],
            device_id=device(d), device_id_type=MESH)

    def image_copy():
        return pltpu.make_async_remote_copy(
            images.at[pl.ds(0, rows)], images.at[pl.ds(rows, rows)], i_sems.at[0], i_sems.at[1],
            device_id=across, device_id_type=MESH)

    def total_copy(c):
        return pltpu.make_async_remote_copy(
            img_send.at[at(c)], img_recv.at[at(c)], x_send.at[c], x_recv.at[c],
            device_id=across, device_id_type=MESH)

    barrier = pltpu.get_barrier_semaphore()
    pl.semaphore_signal(barrier, inc=1, device_id=across, device_id_type=MESH)
    for d in (1, -1):
        @pl.when(has(d))
        def _():
            pl.semaphore_signal(barrier, inc=1, device_id=device(d), device_id_type=MESH)

    @pl.loop(0, CHUNKS)
    def _(c):
        texts[z, at(c)] = unit_rows(txt_ref[at(c)])[2]

    pl.semaphore_wait(barrier, 3 - z // last - (last - z) // last)

    @pl.loop(0, CHUNKS)
    def _(c):
        for d in (1, -1):
            @pl.when(has(d))
            def _():
                gather_copy(d, z, c).start()

    @pl.loop(0, CHUNKS)
    def _(c):
        images[at(c)] = unit_rows(img_ref[at(c)])[2]

    image_copy().start()

    own_images = images[pl.ds(0, rows)]
    own_texts = texts[z]
    logits = scale * dot_last(own_texts, own_images) + bias
    places = lax.broadcasted_iota(jnp.int32, logits.shape, 0)
    sign = jnp.where(places == pos_ref[...], 1.0, -1.0).astype(jnp.float32)
    coefficient = (-sign * scale * jax.nn.sigmoid(-sign * logits)).astype(jnp.bfloat16)
    parts[z] = jnp.dot(coefficient, own_images, preferred_element_type=jnp.float32)
    img_total[pl.ds(0, rows)] = dot_first(coefficient, own_texts)

    def arrive(t, c):
        for d in (1, -1):
            j = z - d * (t + 1)

            @pl.when((j >= 0) & (j <= last))
            def _():
                gather_copy(d, j, c).wait_recv()

                @pl.when(has(d))
                def _():
                    gather_copy(d, j, c).start()

    def meet(t, c):
        @pl.loop(0, 2)
        def _(q):
            j = z + (2 * q - 1) * (t + 1)

            @pl.when((j >= 0) & (j <= last))
            def _():
                both = images[...]
                logits = scale * dot_last(texts[j, at(c)], both) + bias
                coefficient = (scale * jax.nn.sigmoid(logits)).astype(jnp.bfloat16)
                coefs[j, at(c)] = coefficient
                parts[j, at(c)] = jnp.dot(coefficient, both, preferred_element_type=jnp.float32)

    def give_back(t, c):
        for d, j in ((-1, last - t), (1, t)):
            @pl.when((j - z) * d > 0)
            def _():
                @pl.when(has(-d))
                def _():
                    return_copy(d, j, c).wait_recv()
                    parts[j, at(c)] += back[side(d), j, at(c)].astype(jnp.float32)

                back_send[j, at(c)] = parts[j, at(c)].astype(jnp.bfloat16)
                return_copy(d, j, c).start()

    def add_images(j):
        img_total[...] += dot_first(coefs[j], texts[j])

    @pl.loop(0, CHUNKS)
    def _(c):
        arrive(0, c)

    image_copy().wait_recv()
    their_images = images[pl.ds(rows, rows)]
    own_texts = texts[z]
    logits = scale * dot_last(own_texts, their_images) + bias
    coefficient = (scale * jax.nn.sigmoid(logits)).astype(jnp.bfloat16)
    parts[z] += jnp.dot(coefficient, their_images, preferred_element_type=jnp.float32)
    img_total[pl.ds(rows, rows)] = dot_first(coefficient, own_texts)

    @pl.loop(0, CHUNKS)
    def _(c):
        meet(0, c)
        give_back(1, c)
        arrive(1, c)
        meet(1, c)

    @pl.loop(0, CHUNKS)
    def _(c):
        give_back(2, c)
        arrive(2, c)
        meet(2, c)

        @pl.when((c - z) * (c - z) % 9 > 0)
        def _():
            add_images(c)

    @pl.loop(0, 2)
    def _(q):
        @pl.when(z == last * q)
        def _():
            add_images(last - last * q)

    @pl.loop(0, CHUNKS)
    def _(c):
        img_send[at(c)] = img_total[pl.ds(pl.multiple_of(rows + c * piece, piece), piece)].astype(
            jnp.bfloat16
        )
        total_copy(c).start()

    @pl.loop(0, CHUNKS)
    def _(c):
        give_back(3, c)

    @pl.loop(0, CHUNKS)
    def _(c):
        for d in (1, -1):
            @pl.when(has(-d))
            def _():
                return_copy(d, z, c).wait_recv()
                parts[z, at(c)] += back[side(d), z, at(c)].astype(jnp.float32)

        values, inverse, _ = unit_rows(txt_ref[at(c)])
        txt_out[at(c)] = unit_back(values, inverse, parts[z, at(c)])

    @pl.loop(0, CHUNKS)
    def _(c):
        total_copy(c).wait_recv()
        values, inverse, _ = unit_rows(img_ref[at(c)])
        total = img_total[at(c)] + img_recv[at(c)].astype(jnp.float32)
        img_out[at(c)] = unit_back(values, inverse, total)

    image_copy().wait_send()

    @pl.loop(0, CHUNKS)
    def _(c):
        total_copy(c).wait_send()

        @pl.loop(0, STEPS)
        def _(j):
            for d in (1, -1):
                @pl.when(((z - j) * d >= 0) & has(d))
                def _():
                    gather_copy(d, j, c).wait_send()

                @pl.when((j - z) * d > 0)
                def _():
                    return_copy(d, j, c).wait_send()


def line_plan(image_embeds, text_embeds, positives, logit_scale, logit_bias):
    rows, width = image_embeds.shape
    vmem = pl.BlockSpec(memory_space=pltpu.VMEM)
    smem = pl.BlockSpec(memory_space=pltpu.SMEM)
    grad = jax.ShapeDtypeStruct((rows, width), jnp.float32)
    dma = pltpu.SemaphoreType.DMA
    half = functools.partial(pltpu.VMEM, dtype=jnp.bfloat16)
    full = functools.partial(pltpu.VMEM, dtype=jnp.float32)
    return pl.pallas_call(
        line_kernel,
        out_shape=(grad, grad),
        in_specs=[vmem, vmem, vmem, smem, smem],
        out_specs=(vmem, vmem),
        scratch_shapes=[
            half((2 * rows, width)),
            half((STEPS, rows, width)),
            half((STEPS, rows, 2 * rows)),
            full((STEPS, rows, width)),
            full((2 * rows, width)),
            half((2, STEPS, rows, width)),
            half((STEPS, rows, width)),
            half((rows, width)),
            half((rows, width)),
            dma((2,)),
            dma((2, STEPS, CHUNKS)),
            dma((STEPS, CHUNKS)),
            dma((2, STEPS, CHUNKS)),
            dma((2, STEPS, CHUNKS)),
            dma((CHUNKS,)),
            dma((CHUNKS,)),
        ],
        compiler_params=pltpu.CompilerParams(
            collective_id=0, has_side_effects=True, vmem_limit_bytes=48 * 2**20
        ),
        cost_estimate=pl.CostEstimate(
            flops=48 * rows * rows * width, bytes_accessed=12 * rows * width, transcendentals=0
        ),
    )(image_embeds, text_embeds, positives, logit_scale, logit_bias)


def solution(mesh):
    whole_line = mesh.shape["blk"] == 2 * STEPS
    return jax.shard_map(
        line_plan if whole_line else window_plan,
        mesh=mesh,
        in_specs=(
            P(("grp", "blk"), None),
            P(("grp", "blk"), None),
            P(("grp", "blk"), None),
            P(),
            P(),
        ),
        out_specs=(P(("grp", "blk"), None), P(("grp", "blk"), None)),
        check_vma=False,
    )
```

time: 339 us -> 97.1 us (0.29)
  waiting for transfers between devices: 311 us -> 0 us
  Pallas kernels: 0 us -> 88.9 us
  matrix products: 9.65 us -> 0 us
  starting transfers between devices: 8.92 us -> 0 us
  other arithmetic: 6.55 us -> 0 us
  local copies, waits for them, and re-layouts: 0.09 us -> 4.83 us
    ppermute x9 -> x0, waiting for transfers between devices: 311 us -> none  [the longest x7 280 us: shifted(): return lax.ppermute(value, axis, pairs)]
    pallas_call x0 -> x1, Pallas kernels: none -> 88.9 us  [line_plan(): pl.pallas_call(line_kernel, out_shape=(grad, grad), in_specs=[vmem, vmem,...]
    dot_general x24 -> x0, matrix products: 9.65 us -> none  [the longest x8 3.38 us: column_product(): lax.dot_general(coefficient, rows, (((0,), (0,)), ((), ())), preferred_el...]
    ppermute x9 -> x0, starting transfers between devices: 8.92 us -> none  [the longest x7 5.01 us: shifted(): return lax.ppermute(value, axis, pairs)]
    unnamed x6 -> x8, local copies, waits for them, and re-layouts: 0.01 us -> 4.83 us
  transfers between devices with their start and end apart: 9 -> 0, of which waited for: 6 -> 0; matrix products, arithmetic and copies ran while one was open for 2% -> 0% of each run, Pallas kernels for 0% -> 0%
where the time goes in v1:
time: 97.1 us; the launch traced here: 95.6 us
  Pallas kernels  88.9 us (92%)
  local copies, waits for them, and re-layouts  4.83 us (5%)
  between operations  1.94 us (2%)
    pallas_call x1, Pallas kernels, line_plan(): pl.pallas_call(line_kernel, out_shape=(grad, grad), in_specs=[vmem, vmem,...  88.9 us
    unnamed x8, local copies, waits for them, and re-layouts  4.83 us

profile of v1, /device:TPU:0, one launch (start us, length us, event | category | flops | bytes accessed | tf_op | source)
XLA Modules:
  0.0 95.6 jit_solution(17902592718252079388)
XLA Ops:
  1.9 0.0 copy-start
  1.9 1.1 %copy-done = bf16[256,1152]{1,0:T(8,128)(2,1)S(1)} copy-done((bf16[256,1152]{1,0:T(8,128)(2,1)S(1)}, bf16[256,1152]{1,0:T(8,128)(2,1)}, u32[]{:S(2)}) %copy-start) | copy-done | bytes 589848
  3.0 0.0 copy-start.1
  3.0 1.1 %copy-done.1 = bf16[256,1152]{1,0:T(8,128)(2,1)S(1)} copy-done((bf16[256,1152]{1,0:T(8,128)(2,1)S(1)}, bf16[256,1152]{1,0:T(8,128)(2,1)}, u32[]{:S(2)}) %copy-start.1) | copy-done | bytes 589848
  4.1 0.0 copy-start.2
  4.1 0.7 copy-done.2
  4.7 88.9 %shard_map.68 = (f32[256,1152]{1,0:T(8,128)S(1)}, f32[256,1152]{1,0:T(8,128)S(1)}) custom-call(bf16[256,1152]{1,0:T(8,128)(2,1)S(1)} %copy-done, bf16[256,1152]{1,0:T(8,128)(2,1)S(1)} %copy-done.1, s32[1,256]{1,0:T(1,128)S(1)} %copy-done.2, f32[1]{0:T(128)S(6)} %copy.9.scale_ref, f32[1]{0:T(128)S(6)} %copy.10.bias_ref), custom_call_target="tpu_custom_call" | custom-call | flops 3623878656 | bytes 3538944 | tf_op jit(solution)/shard_map/pallas_call | solution.py:293
  93.6 1.0 %copy.11 = f32[256,1152]{1,0:T(8,128)} copy(f32[256,1152]{1,0:T(8,128)S(1)} %get-tuple-element.4) | data formatting | bytes 2359296
  94.6 1.0 %copy.12 = f32[256,1152]{1,0:T(8,128)} copy(f32[256,1152]{1,0:T(8,128)S(1)} %get-tuple-element.5) | data formatting | bytes 2359296
Async XLA Ops:
  1.9 1.1 %copy-start = (bf16[256,1152]{1,0:T(8,128)(2,1)S(1)}, bf16[256,1152]{1,0:T(8,128)(2,1)}, u32[]{:S(2)}) copy-start(bf16[256,1152]{1,0:T(8,128)(2,1)} %img_ref.1) | copy-start | bytes 1769476
  3.0 1.1 %copy-start.1 = (bf16[256,1152]{1,0:T(8,128)(2,1)S(1)}, bf16[256,1152]{1,0:T(8,128)(2,1)}, u32[]{:S(2)}) copy-start(bf16[256,1152]{1,0:T(8,128)(2,1)} %txt_ref.1) | copy-start | bytes 1769476
  4.1 0.7 copy-start.2

commit v2 on v1

--- a/solution.py
+++ b/solution.py
@@ -8,7 +8,10 @@
 from jax.sharding import PartitionSpec as P
 
 STEPS = 4
-CHUNKS = 4
+CHUNKS = 8
+AHEAD = 2
+LAG = 1
+HOLD = 4
 MESH = pl.DeviceIdType.MESH
 
 
@@ -125,6 +128,13 @@
             img_send.at[at(c)], img_recv.at[at(c)], x_send.at[c], x_recv.at[c],
             device_id=across, device_id_type=MESH)
 
+    inward = 1 - 2 * (2 * z // STEPS)
+    middle = z * (last - z) // (last - 1)
+    early = CHUNKS - AHEAD
+
+    def turned(i):
+        return (i + early) % CHUNKS
+
     barrier = pltpu.get_barrier_semaphore()
     pl.semaphore_signal(barrier, inc=1, device_id=across, device_id_type=MESH)
     for d in (1, -1):
@@ -136,14 +146,20 @@
     def _(c):
         texts[z, at(c)] = unit_rows(txt_ref[at(c)])[2]
 
-    pl.semaphore_wait(barrier, 3 - z // last - (last - z) // last)
-
-    @pl.loop(0, CHUNKS)
-    def _(c):
-        for d in (1, -1):
-            @pl.when(has(d))
-            def _():
-                gather_copy(d, z, c).start()
+    pl.semaphore_wait(barrier, 2 + middle)
+
+    @pl.when(middle == 0)
+    def _():
+        @pl.loop(0, CHUNKS)
+        def _(c):
+            gather_copy(inward, z, c).start()
+
+    @pl.when(middle == 1)
+    def _():
+        @pl.loop(early, CHUNKS)
+        def _(c):
+            gather_copy(inward, z, c).start()
+            gather_copy(-inward, z, c).start()
 
     @pl.loop(0, CHUNKS)
     def _(c):
@@ -160,49 +176,52 @@
     parts[z] = jnp.dot(coefficient, own_images, preferred_element_type=jnp.float32)
     img_total[pl.ds(0, rows)] = dot_first(coefficient, own_texts)
 
-    def arrive(t, c):
-        for d in (1, -1):
-            j = z - d * (t + 1)
-
-            @pl.when((j >= 0) & (j <= last))
-            def _():
-                gather_copy(d, j, c).wait_recv()
-
-                @pl.when(has(d))
-                def _():
-                    gather_copy(d, j, c).start()
-
-    def meet(t, c):
-        @pl.loop(0, 2)
-        def _(q):
-            j = z + (2 * q - 1) * (t + 1)
-
-            @pl.when((j >= 0) & (j <= last))
-            def _():
-                both = images[...]
-                logits = scale * dot_last(texts[j, at(c)], both) + bias
-                coefficient = (scale * jax.nn.sigmoid(logits)).astype(jnp.bfloat16)
-                coefs[j, at(c)] = coefficient
-                parts[j, at(c)] = jnp.dot(coefficient, both, preferred_element_type=jnp.float32)
-
-    def give_back(t, c):
-        for d, j in ((-1, last - t), (1, t)):
-            @pl.when((j - z) * d > 0)
-            def _():
-                @pl.when(has(-d))
-                def _():
-                    return_copy(d, j, c).wait_recv()
-                    parts[j, at(c)] += back[side(d), j, at(c)].astype(jnp.float32)
-
-                back_send[j, at(c)] = parts[j, at(c)].astype(jnp.bfloat16)
-                return_copy(d, j, c).start()
+    def pass_on(d, j, c):
+        gather_copy(d, j, c).wait_recv()
+        gather_copy(d, j, c).start()
+
+    def meet(j, c):
+        both = images[...]
+        logits = scale * dot_last(texts[j, at(c)], both) + bias
+        coefficient = (scale * jax.nn.sigmoid(logits)).astype(jnp.bfloat16)
+        coefs[j, at(c)] = coefficient
+        parts[j, at(c)] = jnp.dot(coefficient, both, preferred_element_type=jnp.float32)
+
+    def give_back(d, j, c):
+        back_send[j, at(c)] = parts[j, at(c)].astype(jnp.bfloat16)
+        return_copy(d, j, c).start()
+
+    def add_back(d, j, c):
+        return_copy(d, j, c).wait_recv()
+        total = parts[j, at(c)] + back[side(d), j, at(c)].astype(jnp.float32)
+        back_send[j, at(c)] = total.astype(jnp.bfloat16)
+        return_copy(d, j, c).start()
 
     def add_images(j):
         img_total[...] += dot_first(coefs[j], texts[j])
 
-    @pl.loop(0, CHUNKS)
-    def _(c):
-        arrive(0, c)
+    def send_total():
+        @pl.loop(0, CHUNKS)
+        def _(c):
+            theirs = pl.ds(pl.multiple_of(rows + c * piece, piece), piece)
+            img_send[at(c)] = img_total[theirs].astype(jnp.bfloat16)
+            total_copy(c).start()
+
+    @pl.when(middle == 1)
+    def _():
+        @pl.loop(0, CHUNKS + LAG)
+        def _(i):
+            @pl.when(i < CHUNKS)
+            def _():
+                pass_on(inward, z - inward, i)
+
+            @pl.when(i >= LAG)
+            def _():
+                pass_on(-inward, z + 2 * inward, i - LAG)
+
+        @pl.loop(0, early)
+        def _(c):
+            gather_copy(inward, z, c).start()
 
     image_copy().wait_recv()
     their_images = images[pl.ds(rows, rows)]
@@ -212,42 +231,62 @@
     parts[z] += jnp.dot(coefficient, their_images, preferred_element_type=jnp.float32)
     img_total[pl.ds(rows, rows)] = dot_first(coefficient, own_texts)
 
-    @pl.loop(0, CHUNKS)
-    def _(c):
-        meet(0, c)
-        give_back(1, c)
-        arrive(1, c)
-        meet(1, c)
-
-    @pl.loop(0, CHUNKS)
-    def _(c):
-        give_back(2, c)
-        arrive(2, c)
-        meet(2, c)
-
-        @pl.when((c - z) * (c - z) % 9 > 0)
-        def _():
-            add_images(c)
-
-    @pl.loop(0, 2)
-    def _(q):
-        @pl.when(z == last * q)
-        def _():
-            add_images(last - last * q)
-
-    @pl.loop(0, CHUNKS)
-    def _(c):
-        img_send[at(c)] = img_total[pl.ds(pl.multiple_of(rows + c * piece, piece), piece)].astype(
-            jnp.bfloat16
-        )
-        total_copy(c).start()
-
-    @pl.loop(0, CHUNKS)
-    def _(c):
-        give_back(3, c)
-
-    @pl.loop(0, CHUNKS)
-    def _(c):
+    @pl.when(middle == 0)
+    def _():
+        @pl.loop(0, (STEPS - 1) * CHUNKS)
+        def _(i):
+            c = turned(i)
+            hops = (last - (i + early) // CHUNKS) % last + 1
+            j = z + hops * inward
+            gather_copy(-inward, j, c).wait_recv()
+            meet(j, c)
+            give_back(inward, j, c)
+
+            @pl.when((c == CHUNKS - 1) & (i >= CHUNKS))
+            def _():
+                add_images(j)
+
+        add_images(z + inward)
+        send_total()
+
+    @pl.when(middle == 1)
+    def _():
+        @pl.loop(0, CHUNKS + HOLD)
+        def _(i):
+            @pl.when(i < CHUNKS)
+            def _():
+                pass_on(-inward, z + inward, turned(i))
+
+                @pl.when(i == CHUNKS - 1)
+                def _():
+                    @pl.loop(0, early)
+                    def _(c):
+                        gather_copy(-inward, z, c).start()
+
+                meet(z - inward, i)
+                meet(z + 2 * inward, i)
+
+            @pl.when(i >= HOLD)
+            def _():
+                add_back(inward, z + 2 * inward, i - HOLD)
+                meet(z + inward, turned(i - HOLD))
+
+        @pl.loop(0, STEPS)
+        def _(j):
+            @pl.when(j != z)
+            def _():
+                add_images(j)
+
+        send_total()
+
+        @pl.loop(0, CHUNKS)
+        def _(c):
+            add_back(inward, z + inward, c)
+            add_back(-inward, z - inward, c)
+
+    @pl.loop(0, CHUNKS)
+    def _(i):
+        c = (i + early * middle) % CHUNKS
         for d in (1, -1):
             @pl.when(has(-d))
             def _():

time: 97.1 us -> 72.4 us (0.75); the launches traced: 95.6 us -> 72.1 us
  Pallas kernels: 88.9 us -> 65.4 us
    pallas_call x1, Pallas kernels: 88.9 us -> 65.4 us  [line_plan(): pl.pallas_call(line_kernel, out_shape=(grad, grad), in_specs=[vmem, vmem,...]
where the time goes in v2:
time: 72.4 us; the launch traced here: 72.1 us
  Pallas kernels  65.4 us (90%)
  local copies, waits for them, and re-layouts  4.83 us (7%)
  between operations  1.94 us (3%)
    pallas_call x1, Pallas kernels, line_plan(): pl.pallas_call(line_kernel, out_shape=(grad, grad), in_specs=[vmem, vmem,...  65.4 us
    unnamed x8, local copies, waits for them, and re-layouts  4.83 us

profile of v2, /device:TPU:0, one launch (start us, length us, event | category | flops | bytes accessed | tf_op | source)
XLA Modules:
  0.0 72.1 jit_solution(3569917194310192214)
XLA Ops:
  1.9 0.0 copy-start
  1.9 1.1 %copy-done = bf16[256,1152]{1,0:T(8,128)(2,1)S(1)} copy-done((bf16[256,1152]{1,0:T(8,128)(2,1)S(1)}, bf16[256,1152]{1,0:T(8,128)(2,1)}, u32[]{:S(2)}) %copy-start) | copy-done | bytes 589848
  3.0 0.0 copy-start.1
  3.0 1.1 %copy-done.1 = bf16[256,1152]{1,0:T(8,128)(2,1)S(1)} copy-done((bf16[256,1152]{1,0:T(8,128)(2,1)S(1)}, bf16[256,1152]{1,0:T(8,128)(2,1)}, u32[]{:S(2)}) %copy-start.1) | copy-done | bytes 589848
  4.1 0.0 copy-start.2
  4.1 0.7 copy-done.2
  4.7 65.4 %shard_map.68 = (f32[256,1152]{1,0:T(8,128)S(1)}, f32[256,1152]{1,0:T(8,128)S(1)}) custom-call(bf16[256,1152]{1,0:T(8,128)(2,1)S(1)} %copy-done, bf16[256,1152]{1,0:T(8,128)(2,1)S(1)} %copy-done.1, s32[1,256]{1,0:T(1,128)S(1)} %copy-done.2, f32[1]{0:T(128)S(6)} %copy.9.scale_ref, f32[1]{0:T(128)S(6)} %copy.10.bias_ref), custom_call_target="tpu_custom_call" | custom-call | flops 3623878656 | bytes 3538944 | tf_op jit(solution)/shard_map/pallas_call | solution.py:332
  70.1 1.0 %copy.11 = f32[256,1152]{1,0:T(8,128)} copy(f32[256,1152]{1,0:T(8,128)S(1)} %get-tuple-element.4) | data formatting | bytes 2359296
  71.1 1.0 %copy.12 = f32[256,1152]{1,0:T(8,128)} copy(f32[256,1152]{1,0:T(8,128)S(1)} %get-tuple-element.5) | data formatting | bytes 2359296
Async XLA Ops:
  1.9 1.1 %copy-start = (bf16[256,1152]{1,0:T(8,128)(2,1)S(1)}, bf16[256,1152]{1,0:T(8,128)(2,1)}, u32[]{:S(2)}) copy-start(bf16[256,1152]{1,0:T(8,128)(2,1)} %img_ref.1) | copy-start | bytes 1769476
  3.0 1.1 %copy-start.1 = (bf16[256,1152]{1,0:T(8,128)(2,1)S(1)}, bf16[256,1152]{1,0:T(8,128)(2,1)}, u32[]{:S(2)}) copy-start(bf16[256,1152]{1,0:T(8,128)(2,1)} %txt_ref.1) | copy-start | bytes 1769476
  4.1 0.7 copy-start.2

commit v3 on v2

--- a/solution.py
+++ b/solution.py
@@ -9,9 +9,10 @@
 
 STEPS = 4
 CHUNKS = 8
-AHEAD = 2
-LAG = 1
-HOLD = 4
+AHEAD_IN = 2
+AHEAD_OUT = 5
+LAG = 2
+HOLD = 5
 MESH = pl.DeviceIdType.MESH
 
 
@@ -130,10 +131,8 @@
 
     inward = 1 - 2 * (2 * z // STEPS)
     middle = z * (last - z) // (last - 1)
-    early = CHUNKS - AHEAD
-
-    def turned(i):
-        return (i + early) % CHUNKS
+    early = CHUNKS - AHEAD_IN
+    early_out = CHUNKS - AHEAD_OUT
 
     barrier = pltpu.get_barrier_semaphore()
     pl.semaphore_signal(barrier, inc=1, device_id=across, device_id_type=MESH)
@@ -144,9 +143,11 @@
 
     @pl.loop(0, CHUNKS)
     def _(c):
+        images[at(c)] = unit_rows(img_ref[at(c)])[2]
         texts[z, at(c)] = unit_rows(txt_ref[at(c)])[2]
 
     pl.semaphore_wait(barrier, 2 + middle)
+    image_copy().start()
 
     @pl.when(middle == 0)
     def _():
@@ -159,13 +160,10 @@
         @pl.loop(early, CHUNKS)
         def _(c):
             gather_copy(inward, z, c).start()
+
+        @pl.loop(early_out, CHUNKS)
+        def _(c):
             gather_copy(-inward, z, c).start()
-
-    @pl.loop(0, CHUNKS)
-    def _(c):
-        images[at(c)] = unit_rows(img_ref[at(c)])[2]
-
-    image_copy().start()
 
     own_images = images[pl.ds(0, rows)]
     own_texts = texts[z]
@@ -224,24 +222,29 @@
             gather_copy(inward, z, c).start()
 
     image_copy().wait_recv()
-    their_images = images[pl.ds(rows, rows)]
-    own_texts = texts[z]
-    logits = scale * dot_last(own_texts, their_images) + bias
-    coefficient = (scale * jax.nn.sigmoid(logits)).astype(jnp.bfloat16)
-    parts[z] += jnp.dot(coefficient, their_images, preferred_element_type=jnp.float32)
-    img_total[pl.ds(rows, rows)] = dot_first(coefficient, own_texts)
+    def meet_theirs():
+        their_images = images[pl.ds(rows, rows)]
+        own_texts = texts[z]
+        logits = scale * dot_last(own_texts, their_images) + bias
+        coefficient = (scale * jax.nn.sigmoid(logits)).astype(jnp.bfloat16)
+        parts[z] += jnp.dot(coefficient, their_images, preferred_element_type=jnp.float32)
+        img_total[pl.ds(rows, rows)] = dot_first(coefficient, own_texts)
 
     @pl.when(middle == 0)
     def _():
         @pl.loop(0, (STEPS - 1) * CHUNKS)
         def _(i):
-            c = turned(i)
-            hops = (last - (i + early) // CHUNKS) % last + 1
+            c = (i + early_out) % CHUNKS
+            hops = (last - (i + early_out) // CHUNKS) % last + 1
             j = z + hops * inward
             gather_copy(-inward, j, c).wait_recv()
             meet(j, c)
             give_back(inward, j, c)
 
+            @pl.when(i == AHEAD_OUT)
+            def _():
+                meet_theirs()
+
             @pl.when((c == CHUNKS - 1) & (i >= CHUNKS))
             def _():
                 add_images(j)
@@ -251,15 +254,17 @@
 
     @pl.when(middle == 1)
     def _():
+        meet_theirs()
+
         @pl.loop(0, CHUNKS + HOLD)
         def _(i):
             @pl.when(i < CHUNKS)
             def _():
-                pass_on(-inward, z + inward, turned(i))
+                pass_on(-inward, z + inward, (i + early) % CHUNKS)
 
                 @pl.when(i == CHUNKS - 1)
                 def _():
-                    @pl.loop(0, early)
+                    @pl.loop(0, early_out)
                     def _(c):
                         gather_copy(-inward, z, c).start()
 
@@ -269,7 +274,7 @@
             @pl.when(i >= HOLD)
             def _():
                 add_back(inward, z + 2 * inward, i - HOLD)
-                meet(z + inward, turned(i - HOLD))
+                meet(z + inward, (i - HOLD + early) % CHUNKS)
 
         @pl.loop(0, STEPS)
         def _(j):
@@ -286,7 +291,7 @@
 
     @pl.loop(0, CHUNKS)
     def _(i):
-        c = (i + early * middle) % CHUNKS
+        c = (i + early_out * middle) % CHUNKS
         for d in (1, -1):
             @pl.when(has(-d))
             def _():

time: 72.4 us -> 68.8 us (0.950)
  Pallas kernels: 65.4 us -> 61.3 us
    pallas_call x1, Pallas kernels: 65.4 us -> 61.3 us  [line_plan(): pl.pallas_call(line_kernel, out_shape=(grad, grad), in_specs=[vmem, vmem,...]
where the time goes in v3:
time: 68.8 us; the launch traced here: 68.1 us
  Pallas kernels  61.3 us (89%)
  local copies, waits for them, and re-layouts  4.83 us (7%)
  between operations  1.94 us (3%)
    pallas_call x1, Pallas kernels, line_plan(): pl.pallas_call(line_kernel, out_shape=(grad, grad), in_specs=[vmem, vmem,...  61.3 us
    unnamed x8, local copies, waits for them, and re-layouts  4.83 us

profile of v3, /device:TPU:0, one launch (start us, length us, event | category | flops | bytes accessed | tf_op | source)
XLA Modules:
  0.0 68.1 jit_solution(5396540772324042981)
XLA Ops:
  1.9 0.0 copy-start
  1.9 1.1 %copy-done = bf16[256,1152]{1,0:T(8,128)(2,1)S(1)} copy-done((bf16[256,1152]{1,0:T(8,128)(2,1)S(1)}, bf16[256,1152]{1,0:T(8,128)(2,1)}, u32[]{:S(2)}) %copy-start) | copy-done | bytes 589848
  3.0 0.0 copy-start.1
  3.0 1.1 %copy-done.1 = bf16[256,1152]{1,0:T(8,128)(2,1)S(1)} copy-done((bf16[256,1152]{1,0:T(8,128)(2,1)S(1)}, bf16[256,1152]{1,0:T(8,128)(2,1)}, u32[]{:S(2)}) %copy-start.1) | copy-done | bytes 589848
  4.1 0.0 copy-start.2
  4.1 0.7 copy-done.2
  4.7 61.3 %shard_map.68 = (f32[256,1152]{1,0:T(8,128)S(1)}, f32[256,1152]{1,0:T(8,128)S(1)}) custom-call(bf16[256,1152]{1,0:T(8,128)(2,1)S(1)} %copy-done, bf16[256,1152]{1,0:T(8,128)(2,1)S(1)} %copy-done.1, s32[1,256]{1,0:T(1,128)S(1)} %copy-done.2, f32[1]{0:T(128)S(6)} %copy.9.scale_ref, f32[1]{0:T(128)S(6)} %copy.10.bias_ref), custom_call_target="tpu_custom_call" | custom-call | flops 3623878656 | bytes 3538944 | tf_op jit(solution)/shard_map/pallas_call | solution.py:337
  66.1 1.0 %copy.11 = f32[256,1152]{1,0:T(8,128)} copy(f32[256,1152]{1,0:T(8,128)S(1)} %get-tuple-element.4) | data formatting | bytes 2359296
  67.1 1.0 %copy.12 = f32[256,1152]{1,0:T(8,128)} copy(f32[256,1152]{1,0:T(8,128)S(1)} %get-tuple-element.5) | data formatting | bytes 2359296
Async XLA Ops:
  1.9 1.1 %copy-start = (bf16[256,1152]{1,0:T(8,128)(2,1)S(1)}, bf16[256,1152]{1,0:T(8,128)(2,1)}, u32[]{:S(2)}) copy-start(bf16[256,1152]{1,0:T(8,128)(2,1)} %img_ref.1) | copy-start | bytes 1769476
  3.0 1.1 %copy-start.1 = (bf16[256,1152]{1,0:T(8,128)(2,1)S(1)}, bf16[256,1152]{1,0:T(8,128)(2,1)}, u32[]{:S(2)}) copy-start(bf16[256,1152]{1,0:T(8,128)(2,1)} %txt_ref.1) | copy-start | bytes 1769476
  4.1 0.7 copy-start.2

commit v4 on v3

--- a/solution.py
+++ b/solution.py
@@ -141,10 +141,11 @@
         def _():
             pl.semaphore_signal(barrier, inc=1, device_id=device(d), device_id_type=MESH)
 
-    @pl.loop(0, CHUNKS)
-    def _(c):
-        images[at(c)] = unit_rows(img_ref[at(c)])[2]
-        texts[z, at(c)] = unit_rows(txt_ref[at(c)])[2]
+    @pl.loop(0, 2)
+    def _(i):
+        half = pl.ds(pl.multiple_of(i * (rows // 2), rows // 2), rows // 2)
+        images[half] = unit_rows(img_ref[half])[2]
+        texts[z, half] = unit_rows(txt_ref[half])[2]
 
     pl.semaphore_wait(barrier, 2 + middle)
     image_copy().start()
@@ -276,18 +277,24 @@
                 add_back(inward, z + 2 * inward, i - HOLD)
                 meet(z + inward, (i - HOLD + early) % CHUNKS)
 
-        @pl.loop(0, STEPS)
-        def _(j):
-            @pl.when(j != z)
-            def _():
-                add_images(j)
-
+            @pl.when(i >= HOLD + LAG)
+            def _():
+                add_back(-inward, z - inward, i - HOLD - LAG)
+
+            @pl.when((i == CHUNKS) | (i == CHUNKS + 2))
+            def _():
+                add_images(z - inward + (i - CHUNKS) // 2 * 3 * inward)
+
+        add_images(z + inward)
         send_total()
 
         @pl.loop(0, CHUNKS)
         def _(c):
             add_back(inward, z + inward, c)
-            add_back(-inward, z - inward, c)
+
+            @pl.when(c < LAG)
+            def _():
+                add_back(-inward, z - inward, CHUNKS - LAG + c)
 
     @pl.loop(0, CHUNKS)
     def _(i):
@@ -301,12 +308,10 @@
         values, inverse, _ = unit_rows(txt_ref[at(c)])
         txt_out[at(c)] = unit_back(values, inverse, parts[z, at(c)])
 
-    @pl.loop(0, CHUNKS)
-    def _(c):
-        total_copy(c).wait_recv()
-        values, inverse, _ = unit_rows(img_ref[at(c)])
-        total = img_total[at(c)] + img_recv[at(c)].astype(jnp.float32)
-        img_out[at(c)] = unit_back(values, inverse, total)
+        total_copy(i).wait_recv()
+        values, inverse, _ = unit_rows(img_ref[at(i)])
+        total = img_total[at(i)] + img_recv[at(i)].astype(jnp.float32)
+        img_out[at(i)] = unit_back(values, inverse, total)
 
     image_copy().wait_send()
 

time: 68.8 us -> 68.6 us (level)
  no operation moved by 1% of the time
where the time goes in v4:
time: 68.6 us; the launch traced here: 67.8 us
  Pallas kernels  61 us (89%)
  local copies, waits for them, and re-layouts  4.83 us (7%)
  between operations  1.94 us (3%)
    pallas_call x1, Pallas kernels, line_plan(): pl.pallas_call(line_kernel, out_shape=(grad, grad), in_specs=[vmem, vmem,...  61 us
    unnamed x8, local copies, waits for them, and re-layouts  4.83 us

profile of v4, /device:TPU:0, one launch (start us, length us, event | category | flops | bytes accessed | tf_op | source)
XLA Modules:
  0.0 67.8 jit_solution(1096236937768626934)
XLA Ops:
  1.9 0.0 copy-start
  1.9 1.1 %copy-done = bf16[256,1152]{1,0:T(8,128)(2,1)S(1)} copy-done((bf16[256,1152]{1,0:T(8,128)(2,1)S(1)}, bf16[256,1152]{1,0:T(8,128)(2,1)}, u32[]{:S(2)}) %copy-start) | copy-done | bytes 589848
  3.0 0.0 copy-start.1
  3.0 1.1 %copy-done.1 = bf16[256,1152]{1,0:T(8,128)(2,1)S(1)} copy-done((bf16[256,1152]{1,0:T(8,128)(2,1)S(1)}, bf16[256,1152]{1,0:T(8,128)(2,1)}, u32[]{:S(2)}) %copy-start.1) | copy-done | bytes 589848
  4.1 0.0 copy-start.2
  4.1 0.7 copy-done.2
  4.7 61.0 %shard_map.68 = (f32[256,1152]{1,0:T(8,128)S(1)}, f32[256,1152]{1,0:T(8,128)S(1)}) custom-call(bf16[256,1152]{1,0:T(8,128)(2,1)S(1)} %copy-done, bf16[256,1152]{1,0:T(8,128)(2,1)S(1)} %copy-done.1, s32[1,256]{1,0:T(1,128)S(1)} %copy-done.2, f32[1]{0:T(128)S(6)} %copy.9.scale_ref, f32[1]{0:T(128)S(6)} %copy.10.bias_ref), custom_call_target="tpu_custom_call" | custom-call | flops 3623878656 | bytes 3538944 | tf_op jit(solution)/shard_map/pallas_call | solution.py:342
  65.8 1.0 %copy.11 = f32[256,1152]{1,0:T(8,128)} copy(f32[256,1152]{1,0:T(8,128)S(1)} %get-tuple-element.4) | data formatting | bytes 2359296
  66.8 1.0 %copy.12 = f32[256,1152]{1,0:T(8,128)} copy(f32[256,1152]{1,0:T(8,128)S(1)} %get-tuple-element.5) | data formatting | bytes 2359296
Async XLA Ops:
  1.9 1.1 %copy-start = (bf16[256,1152]{1,0:T(8,128)(2,1)S(1)}, bf16[256,1152]{1,0:T(8,128)(2,1)}, u32[]{:S(2)}) copy-start(bf16[256,1152]{1,0:T(8,128)(2,1)} %img_ref.1) | copy-start | bytes 1769476
  3.0 1.1 %copy-start.1 = (bf16[256,1152]{1,0:T(8,128)(2,1)S(1)}, bf16[256,1152]{1,0:T(8,128)(2,1)}, u32[]{:S(2)}) copy-start(bf16[256,1152]{1,0:T(8,128)(2,1)} %txt_ref.1) | copy-start | bytes 1769476
  4.1 0.7 %copy-start.2 = (s32[1,256]{1,0:T(1,128)S(1)}, s32[1,256]{1,0:T(1,128)}, u32[]{:S(2)}) copy-start(s32[1,256]{1,0:T(1,128)} %pos_ref.1) | copy-start | bytes 3076
